TPU v7x, 32 devices: a whole 2x2x4 slice. The times are simulated.
32 devices in a mesh: expert: 4 (over y, x), hidden: 8 (over z, core).
Axes of the slice: x: 2, y: 2, z: 4, core: 2. Of those that a mesh axis runs over, the one named last changes fastest.
Arguments:
- tokens: bfloat16 [192, 6144], P(('expert', 'hidden')), may hold values from -6 to 6
- routes: int32 [192, 2], P(('expert', 'hidden')), may hold values from 0 to 3, all different within a row; in each aligned block of 6 rows (0 to 5, 6 to 11, ...) at most 4 rows name the same one
- gate_probs: float32 [192, 2], P(('expert', 'hidden')), may hold values from 0.1 to 1
- cotangent: bfloat16 [192, 6144], P(('expert', 'hidden')), may hold values from -6 to 6
- w_gate: bfloat16 [4, 6144, 8192], P('expert', None, 'hidden'), may hold values from -0.078125 to 0.078125
- w_up: bfloat16 [4, 6144, 8192], P('expert', None, 'hidden'), may hold values from -0.078125 to 0.078125
- w_down: bfloat16 [4, 8192, 6144], P('expert', 'hidden'), may hold values from -0.0625 to 0.0625
Outputs:
- layer_out: bfloat16 [192, 6144], P(('expert', 'hidden'))
- grad_tokens: bfloat16 [192, 6144], P(('expert', 'hidden'))
- grad_gate: bfloat16 [4, 6144, 8192], P('expert', None, 'hidden')
- grad_up: bfloat16 [4, 6144, 8192], P('expert', None, 'hidden')
- grad_down: bfloat16 [4, 8192, 6144], P('expert', 'hidden')
Inputs may be any that keep to these rules, and one draw needn't show every extreme that they name: `routes`: each row names two different experts. Within the tokens of one device (aligned blocks of 6 rows) no expert is named by more than 4 rows, a bound that some block reaches.
All inputs are finite; a program needn't handle non-finite values.
Results may differ from a plain program's by a relative error of at most 0.015.
Values may be sent and summed in bfloat16 or wider, within the bound.
A program may use at most 192 MiB of HBM per device.

v0:
```python
import jax
import jax.numpy as jnp
from jax import lax
from jax.sharding import PartitionSpec as P


def slot_table(route_ids, experts, capacity):
    flat_ids = route_ids.reshape(-1)
    hits = (flat_ids[:, None] == jnp.arange(experts, dtype=jnp.int32)[None, :]).astype(jnp.int32)
    before = jnp.cumsum(hits, axis=0) - hits
    ranks = jnp.sum(before * hits, axis=1)
    slot_ids = flat_ids * capacity + ranks
    table = (slot_ids[:, None] == jnp.arange(experts * capacity, dtype=jnp.int32)[None, :]).astype(
        jnp.float32
    )
    return table.reshape(route_ids.shape[0], 2, experts * capacity)


def on_device(tokens, routes, gate_probs, cotangent, w_gate, w_up, w_down):
    experts = lax.axis_size("expert")
    width = tokens.shape[1]
    capacity = (2 * tokens.shape[0] + experts - 1) // experts + 1
    table = slot_table(routes, experts, capacity)
    placed = jnp.sum(table, axis=1)
    weighted = jnp.sum(table * gate_probs[:, :, None], axis=1)
    send_in = jnp.dot(
        placed.T.astype(jnp.bfloat16), tokens, preferred_element_type=jnp.float32
    ).astype(jnp.bfloat16)
    send_grad = jnp.dot(
        weighted.T, cotangent.astype(jnp.float32), precision=lax.Precision.HIGHEST
    ).astype(jnp.bfloat16)
    send_in = send_in.reshape(experts, capacity, width)
    send_grad = send_grad.reshape(experts, capacity, width)
    grouped = (
        lax.all_gather(send_in[None], "hidden", axis=0, tiled=True),
        lax.all_gather(send_grad[None], "hidden", axis=0, tiled=True),
    )
    arrived = (
        lax.all_to_all(grouped[0], "expert", split_axis=1, concat_axis=1, tiled=True),
        lax.all_to_all(grouped[1], "expert", split_axis=1, concat_axis=1, tiled=True),
    )
    expert_rows = arrived[0].reshape(-1, width)
    grad_rows = arrived[1].reshape(-1, width)
    gate_w = w_gate[0]
    up_w = w_up[0]
    down_w = w_down[0]
    pre_gate = jnp.dot(expert_rows, gate_w, preferred_element_type=jnp.float32)
    pre_up = jnp.dot(expert_rows, up_w, preferred_element_type=jnp.float32)
    sig_gate = jax.nn.sigmoid(pre_gate)
    hidden = (pre_gate * sig_gate * pre_up).astype(jnp.bfloat16)
    summed_out = lax.psum_scatter(
        jnp.dot(hidden, down_w, preferred_element_type=jnp.float32).astype(jnp.bfloat16),
        "hidden",
        scatter_dimension=0,
        tiled=True,
    )
    expert_out = summed_out.reshape(experts, capacity, width)
    returned = lax.all_to_all(expert_out, "expert", split_axis=0, concat_axis=0, tiled=True)
    layer_out = jnp.dot(
        weighted, returned.reshape(-1, width).astype(jnp.float32), precision=lax.Precision.HIGHEST
    ).astype(jnp.bfloat16)
    grad_hidden = jnp.dot(grad_rows, down_w.T, preferred_element_type=jnp.float32)
    grad_pre_gate = (grad_hidden * pre_up * sig_gate * (1.0 + pre_gate * (1.0 - sig_gate))).astype(
        jnp.bfloat16
    )
    grad_pre_up = (grad_hidden * pre_gate * sig_gate).astype(jnp.bfloat16)
    grad_down = jnp.dot(hidden.T, grad_rows, preferred_element_type=jnp.float32).astype(
        jnp.bfloat16
    )
    grad_gate = jnp.dot(expert_rows.T, grad_pre_gate, preferred_element_type=jnp.float32).astype(
        jnp.bfloat16
    )
    grad_up = jnp.dot(expert_rows.T, grad_pre_up, preferred_element_type=jnp.float32).astype(
        jnp.bfloat16
    )
    first = jnp.dot(grad_pre_gate, gate_w.T, preferred_element_type=jnp.float32)
    summed_back = lax.psum_scatter(
        (first + jnp.dot(grad_pre_up, up_w.T, preferred_element_type=jnp.float32)).astype(
            jnp.bfloat16
        ),
        "hidden",
        scatter_dimension=0,
        tiled=True,
    )
    expert_back = summed_back.reshape(experts, capacity, width)
    returned_back = lax.all_to_all(expert_back, "expert", split_axis=0, concat_axis=0, tiled=True)
    grad_tokens = jnp.dot(
        placed,
        returned_back.reshape(-1, width).astype(jnp.float32),
        precision=lax.Precision.HIGHEST,
    ).astype(jnp.bfloat16)
    return (layer_out, grad_tokens, grad_gate[None], grad_up[None], grad_down[None])


def solution(mesh):
    return jax.shard_map(
        on_device,
        mesh=mesh,
        in_specs=(
            P(("expert", "hidden"), None),
            P(("expert", "hidden"), None),
            P(("expert", "hidden"), None),
            P(("expert", "hidden"), None),
            P("expert", None, "hidden"),
            P("expert", None, "hidden"),
            P("expert", "hidden", None),
        ),
        out_specs=(
            P(("expert", "hidden"), None),
            P(("expert", "hidden"), None),
            P("expert", None, "hidden"),
            P("expert", None, "hidden"),
            P("expert", "hidden", None),
        ),
        check_vma=False,
    )
```

profile of v0, /device:TPU:0, one launch (start us, length us, event | category | flops | bytes accessed | tf_op | source)
XLA Modules:
  0.0 226.8 jit_solution(520925246236391324)
XLA Ops:
  7.2 0.0 copy-start
  7.2 0.0 all-gather.3.cloned.1.call-start
  7.2 0.8 copy.30
  8.0 0.1 eq.29
  8.1 0.2 reduce_window_sum.11
  8.3 0.1 reduce_sum.30
  8.4 0.8 copy.32
  9.2 0.1 convert_reduce_fusion
  9.3 0.2 convolution_convert_fusion.1
  9.5 0.8 broadcast_in_dim_reshape.7
  10.3 0.0 all-gather.3.cloned.1.call-update
  10.3 0.0 all-gather.5.cloned.1.call-start
  10.3 1.3 convolution_convert_fusion
  11.7 0.8 broadcast_in_dim_reshape.8
  12.4 0.0 all-gather.5.cloned.1.call-update
  12.4 25.8 %all-gather.3.cloned.1.call-done = bf16[8,4,4,6144]{3,2,1,0:T(4,128)(2,1)} async-done(((bf16[1,4,4,6144]{3,2,1,0:T(4,128)(2,1)}), bf16[8,4,4,6144]{3,2,1,0:T(4,128)(2,1)}) %all-gather.3.cloned.1.call-update) | async-done | bytes 1572880 | tf_op jit(solution)/shard_map/all_gather | solution.py:35
  38.2 3.3 %copy.33 = bf16[8,4,4,6144]{3,2,0,1:T(4,128)(2,1)} copy(bf16[8,4,4,6144]{3,2,1,0:T(4,128)(2,1)} %all-gather.3.cloned.1.call-done) | data formatting | bytes 3145728 | tf_op jit(solution)/shard_map/all_gather | solution.py:35
  41.5 3.6 %all-to-all-start = ((bf16[8,4,4,6144]{3,2,0,1:T(4,128)(2,1)}), bf16[8,4,4,6144]{3,2,0,1:T(4,128)(2,1)S(1)}, u32[]{:S(2)}, u32[]{:S(2)}) async-start(bf16[8,4,4,6144]{3,2,0,1:T(4,128)(2,1)} %copy.33), calls=%async_computation | async-start | bytes 3145728 | tf_op jit(solution)/shard_map/all_to_all | solution.py:39
  45.1 19.9 %all-gather.5.cloned.1.call-done = bf16[8,4,4,6144]{3,2,1,0:T(4,128)(2,1)} async-done(((bf16[1,4,4,6144]{3,2,1,0:T(4,128)(2,1)}), bf16[8,4,4,6144]{3,2,1,0:T(4,128)(2,1)}) %all-gather.5.cloned.1.call-update) | async-done | bytes 1572880 | tf_op jit(solution)/shard_map/all_gather | solution.py:36
  65.0 3.3 %copy.35 = bf16[8,4,4,6144]{3,2,0,1:T(4,128)(2,1)} copy(bf16[8,4,4,6144]{3,2,1,0:T(4,128)(2,1)} %all-gather.5.cloned.1.call-done) | data formatting | bytes 3145728 | tf_op jit(solution)/shard_map/all_gather | solution.py:36
  68.3 4.3 %all-to-all-start.2 = ((bf16[8,4,4,6144]{3,2,0,1:T(4,128)(2,1)}), bf16[8,4,4,6144]{3,2,0,1:T(4,128)(2,1)}, u32[]{:S(2)}, u32[]{:S(2)}) async-start(bf16[8,4,4,6144]{3,2,0,1:T(4,128)(2,1)} %copy.35), calls=%async_computation.3 | async-start | bytes 3145728 | tf_op jit(solution)/shard_map/all_to_all | solution.py:40
  72.6 0.0 reduce-scatter.5.cloned.1.call-start
  72.7 1.9 copy.34
  74.6 2.7 %reshape.48 = bf16[128,6144]{1,0:T(8,128)(2,1)S(1)} reshape(bf16[8,4,4,6144]{3,2,1,0:T(4,128)(2,1)} %copy.34) | data formatting | bytes 3145728 | tf_op jit(solution)/shard_map/reshape | solution.py:42
  77.3 15.4 %all-to-all-done.2 = bf16[8,4,4,6144]{3,2,0,1:T(4,128)(2,1)} async-done(((bf16[8,4,4,6144]{3,2,0,1:T(4,128)(2,1)}), bf16[8,4,4,6144]{3,2,0,1:T(4,128)(2,1)}, u32[]{:S(2)}, u32[]{:S(2)}) %all-to-all-start.2) | async-done | bytes 1572896 | tf_op jit(solution)/shard_map/all_to_all | solution.py:40
  92.6 3.3 %copy.36 = bf16[8,4,4,6144]{3,2,1,0:T(4,128)(2,1)} copy(bf16[8,4,4,6144]{3,2,0,1:T(4,128)(2,1)} %all-to-all-done.2) | data formatting | bytes 3145728 | tf_op jit(solution)/shard_map/all_to_all | solution.py:40
  95.9 2.9 %reshape.51 = bf16[128,6144]{1,0:T(8,128)(2,1)S(1)} reshape(bf16[8,4,4,6144]{3,2,1,0:T(4,128)(2,1)} %copy.36) | data formatting | bytes 3145728 | tf_op jit(solution)/shard_map/reshape | solution.py:43
  98.8 7.2 %fusion.6 = f32[128,1024]{1,0:T(8,128)} fusion(bf16[128,6144]{1,0:T(8,128)(2,1)S(1)} %reshape.48, bf16[1,6144,1024]{2,1,0:T(8,128)(2,1)} %param.12), kind=kOutput, calls=%fused_computation.6 | convolution fusion | flops 1610612736 | bytes 14680064 | tf_op jit(solution)/shard_map/dot_general | solution.py:48
  105.9 9.8 %fusion = f32[128,1024]{1,0:T(8,128)} fusion(bf16[128,6144]{1,0:T(8,128)(2,1)S(1)} %reshape.51, bf16[1,1024,6144]{2,1,0:T(8,128)(2,1)} %param.13), kind=kOutput, calls=%fused_computation | convolution fusion | flops 1610612736 | bytes 14680064 | tf_op jit(solution)/shard_map/dot_general | solution.py:62
  115.7 7.8 %multiply_convert_fusion.1 = (bf16[128,1024]{1,0:T(8,128)(2,1)S(1)}, bf16[128,1024]{1,0:T(8,128)(2,1)}, bf16[128,1024]{1,0:T(8,128)(2,1)}) fusion(f32[128,1024]{1,0:T(8,128)} %fusion, f32[128,1024]{1,0:T(8,128)} %fusion.6, bf16[128,6144]{1,0:T(8,128)(2,1)S(1)} %reshape.48, bf16[1,6144,1024]{2,1,0:T(8,128)(2,1)} %param.11), kind=kOutput, calls=%fused_computation.23 | convolution fusion | flops 1612709888 | bytes 15990784 | tf_op jit(solution)/shard_map/dot_general | solution.py:47
  123.5 6.9 %fusion.4 = f32[128,6144]{1,0:T(8,128)} fusion(bf16[128,1024]{1,0:T(8,128)(2,1)} %get-tuple-element.9, bf16[1,6144,1024]{2,1,0:T(8,128)(2,1)S(1)} %bitcast.49), kind=kOutput, calls=%fused_computation.4 | convolution fusion | flops 1610612736 | bytes 15990784 | tf_op jit(solution)/shard_map/dot_general | solution.py:78
  130.4 11.1 %fusion.15 = bf16[128,6144]{1,0:T(8,128)(2,1)} fusion(f32[128,6144]{1,0:T(8,128)} %fusion.4, bf16[128,1024]{1,0:T(8,128)(2,1)S(1)} %get-tuple-element.7, bf16[1,6144,1024]{2,1,0:T(8,128)(2,1)} %param.11), kind=kOutput, calls=%fused_computation.16 | convolution fusion | flops 1612185600 | bytes 17563648 | tf_op jit(solution)/shard_map/dot_general | solution.py:76
  141.5 0.0 reduce-scatter.5.cloned.1.call-update
  141.5 0.0 reduce-scatter.3.cloned.1.call-start
  141.6 7.7 %fusion.18 = bf16[128,6144]{1,0:T(8,128)(2,1)} fusion(bf16[128,1024]{1,0:T(8,128)(2,1)} %get-tuple-element.8, bf16[1,1024,6144]{2,1,0:T(8,128)(2,1)} %param.13), kind=kOutput, calls=%fused_computation.17 | convolution fusion | flops 1611399168 | bytes 14417920 | tf_op jit(solution)/shard_map/dot_general | solution.py:52
  149.2 0.0 reduce-scatter.3.cloned.1.call-update
  149.2 7.6 %convert_bitcast_fusion.1 = bf16[1,6144,1024]{2,1,0:T(8,128)(2,1)} fusion(bf16[128,6144]{1,0:T(8,128)(2,1)S(1)} %reshape.48, bf16[128,1024]{1,0:T(8,128)(2,1)} %get-tuple-element.9), kind=kOutput, calls=%fused_computation.13 | convolution fusion | flops 1616904192 | bytes 14417920 | tf_op jit(solution)/shard_map/dot_general | solution.py:73
  156.8 6.6 %convert_bitcast_fusion.2 = bf16[1,6144,1024]{2,1,0:T(8,128)(2,1)} fusion(bf16[128,6144]{1,0:T(8,128)(2,1)S(1)} %reshape.48, bf16[128,1024]{1,0:T(8,128)(2,1)S(1)} %get-tuple-element.7), kind=kOutput, calls=%fused_computation.14 | convolution fusion | flops 1616904192 | bytes 14417920 | tf_op jit(solution)/shard_map/dot_general | solution.py:70
  163.4 11.1 %reduce-scatter.5.cloned.1.call-done = bf16[16,6144]{1,0:T(8,128)(2,1)} async-done(((bf16[128,6144]{1,0:T(8,128)(2,1)}), bf16[16,6144]{1,0:T(8,128)(2,1)}) %reduce-scatter.5.cloned.1.call-update) | async-done | bytes 196624 | tf_op jit(solution)/shard_map/reduce_scatter | solution.py:77
  174.6 1.7 reshape.52
  176.3 3.5 %all-to-all-start.3 = ((bf16[4,4,6144]{2,1,0:T(4,128)(2,1)}), bf16[4,4,6144]{2,1,0:T(4,128)(2,1)S(1)}, u32[]{:S(2)}, u32[]{:S(2)}) async-start(bf16[4,4,6144]{2,1,0:T(4,128)(2,1)} %reshape.52), calls=%async_computation.5 | async-start | bytes 393216 | tf_op jit(solution)/shard_map/all_to_all | solution.py:86
  179.8 7.6 %convert_bitcast_fusion = bf16[1,1024,6144]{2,1,0:T(8,128)(2,1)} fusion(bf16[128,1024]{1,0:T(8,128)(2,1)} %get-tuple-element.8, bf16[128,6144]{1,0:T(8,128)(2,1)S(1)} %reshape.51), kind=kOutput, calls=%fused_computation.12 | convolution fusion | flops 1616904192 | bytes 14417920 | tf_op jit(solution)/shard_map/dot_general | solution.py:67
  187.4 21.5 %reduce-scatter.3.cloned.1.call-done = bf16[16,6144]{1,0:T(8,128)(2,1)} async-done(((bf16[128,6144]{1,0:T(8,128)(2,1)}), bf16[16,6144]{1,0:T(8,128)(2,1)}) %reduce-scatter.3.cloned.1.call-update) | async-done | bytes 196624 | tf_op jit(solution)/shard_map/reduce_scatter | solution.py:51
  208.8 1.7 reshape.49
  210.5 3.6 %all-to-all-start.1 = ((bf16[4,4,6144]{2,1,0:T(4,128)(2,1)}), bf16[4,4,6144]{2,1,0:T(4,128)(2,1)S(1)}, u32[]{:S(2)}, u32[]{:S(2)}) async-start(bf16[4,4,6144]{2,1,0:T(4,128)(2,1)} %reshape.49), calls=%async_computation.2 | async-start | bytes 393216 | tf_op jit(solution)/shard_map/all_to_all | solution.py:58
  214.2 0.9 convolution_convert_fusion.2
  215.0 4.3 %all-to-all-done.1 = bf16[4,4,6144]{2,1,0:T(4,128)(2,1)S(1)} async-done(((bf16[4,4,6144]{2,1,0:T(4,128)(2,1)}), bf16[4,4,6144]{2,1,0:T(4,128)(2,1)S(1)}, u32[]{:S(2)}, u32[]{:S(2)}) %all-to-all-start.1) | async-done | bytes 196640 | tf_op jit(solution)/shard_map/all_to_all | solution.py:58
  219.4 0.9 convolution_convert_fusion.3
  (17 shorter events, 0.2 us)
Async XLA Ops:
  7.2 2.1 copy-start
  7.2 31.0 %all-gather.3.cloned.1.call-start = ((), (), s32[]{:S(2)}) async-start(), calls=%async_computation.6 | async-start | bytes 1769472 | tf_op jit(solution)/shard_map/all_gather | solution.py:35
  10.3 54.7 %all-gather.5.cloned.1.call-start = ((), (), s32[]{:S(2)}) async-start(), calls=%async_computation.8 | async-start | bytes 1769472 | tf_op jit(solution)/shard_map/all_gather | solution.py:36
  41.5 26.8 %all-to-all-start = ((bf16[8,4,4,6144]{3,2,0,1:T(4,128)(2,1)}), bf16[8,4,4,6144]{3,2,0,1:T(4,128)(2,1)S(1)}, u32[]{:S(2)}, u32[]{:S(2)}) async-start(bf16[8,4,4,6144]{3,2,0,1:T(4,128)(2,1)} %copy.33), calls=%async_computation | async-start | bytes 3145728 | tf_op jit(solution)/shard_map/all_to_all | solution.py:39
  68.3 24.3 %all-to-all-start.2 = ((bf16[8,4,4,6144]{3,2,0,1:T(4,128)(2,1)}), bf16[8,4,4,6144]{3,2,0,1:T(4,128)(2,1)}, u32[]{:S(2)}, u32[]{:S(2)}) async-start(bf16[8,4,4,6144]{3,2,0,1:T(4,128)(2,1)} %copy.35), calls=%async_computation.3 | async-start | bytes 3145728 | tf_op jit(solution)/shard_map/all_to_all | solution.py:40
  72.6 101.9 %reduce-scatter.5.cloned.1.call-start = ((), (), s32[]{:S(2)}) async-start(), calls=%async_computation.9 | async-start | bytes 1769472 | tf_op jit(solution)/shard_map/reduce_scatter | solution.py:77
  105.9 17.6 %slice-start = ((s8[12582912]{0:T(1024)(128)(4,1)}), s8[4194304]{0:T(1024)(128)(4,1)S(1)}, s32[]{:S(2)}) async-start(s8[12582912]{0:T(1024)(128)(4,1)} %bitcast.48), calls=%async_computation.10 | async-start | bytes 8388608
  105.9 17.6 %slice-start.1 = ((s8[12582912]{0:T(1024)(128)(4,1)}), s8[4194304]{0:T(1024)(128)(4,1)S(1)}, s32[]{:S(2)}) async-start(s8[12582912]{0:T(1024)(128)(4,1)} %bitcast.48), calls=%async_computation.11 | async-start | bytes 8388608
  115.7 7.8 %slice-start.2 = ((s8[12582912]{0:T(1024)(128)(4,1)}), s8[4194304]{0:T(1024)(128)(4,1)S(1)}, s32[]{:S(2)}) async-start(s8[12582912]{0:T(1024)(128)(4,1)} %bitcast.48), calls=%async_computation.12 | async-start | bytes 8388608
  141.5 67.3 %reduce-scatter.3.cloned.1.call-start = ((), (), s32[]{:S(2)}) async-start(), calls=%async_computation.7 | async-start | bytes 1769472 | tf_op jit(solution)/shard_map/reduce_scatter | solution.py:51
  176.3 34.3 %all-to-all-start.3 = ((bf16[4,4,6144]{2,1,0:T(4,128)(2,1)}), bf16[4,4,6144]{2,1,0:T(4,128)(2,1)S(1)}, u32[]{:S(2)}, u32[]{:S(2)}) async-start(bf16[4,4,6144]{2,1,0:T(4,128)(2,1)} %reshape.52), calls=%async_computation.5 | async-start | bytes 393216 | tf_op jit(solution)/shard_map/all_to_all | solution.py:86
  179.7 40.5 %copy-start.1 = (bf16[6,6144]{1,0:T(8,128)(2,1)S(1)}, bf16[6,6144]{1,0:T(8,128)(2,1)}, u32[]{:S(2)}) copy-start(bf16[6,6144]{1,0:T(8,128)(2,1)} %param.7) | copy-start | bytes 221188
  210.5 8.8 %all-to-all-start.1 = ((bf16[4,4,6144]{2,1,0:T(4,128)(2,1)}), bf16[4,4,6144]{2,1,0:T(4,128)(2,1)S(1)}, u32[]{:S(2)}, u32[]{:S(2)}) async-start(bf16[4,4,6144]{2,1,0:T(4,128)(2,1)} %reshape.49), calls=%async_computation.2 | async-start | bytes 393216 | tf_op jit(solution)/shard_map/all_to_all | solution.py:58
Sparse Core Ops, SparseCore 0:
  10.4 27.7 all-gather.2
  40.4 24.5 all-gather.4
  141.6 32.8 reduce-scatter.4
  176.7 32.0 reduce-scatter.2
where the time goes:
time: 228 us; the launch traced here: 227 us
  waiting for transfers between devices  98 us (43%)
  matrix products  75.4 us (33%)
  local copies, waits for them, and re-layouts  23.9 us (10%)
  starting transfers between devices  15.3 us (7%)
  between operations  13.9 us (6%)
    all_gather x1, waiting for transfers between devices, on_device(): lax.all_gather(send_in[None], 'hidden', axis=0, tiled=True)  25.8 us
    reduce_scatter x1, waiting for transfers between devices, on_device(): lax.psum_scatter(jnp.dot(hidden, down_w, preferred_element_type=jnp.float...  21.5 us
    all_gather x1, waiting for transfers between devices, on_device(): lax.all_gather(send_grad[None], 'hidden', axis=0, tiled=True)  19.9 us
    all_to_all x1, waiting for transfers between devices, on_device(): lax.all_to_all(grouped[1], 'expert', split_axis=1, concat_axis=1, tiled=T...  15.4 us
    reduce_scatter x1, waiting for transfers between devices, on_device(): lax.psum_scatter((first + jnp.dot(grad_pre_up, up_w.T, preferred_element_...  11.1 us
    dot_general x1, matrix products, on_device(): first = jnp.dot(grad_pre_gate, gate_w.T, preferred_element_type=jnp.float32)  11.1 us
    dot_general x1, matrix products, on_device(): jnp.dot(grad_rows, down_w.T, preferred_element_type=jnp.float32)  9.76 us
    dot_general x1, matrix products, on_device(): pre_gate = jnp.dot(expert_rows, gate_w, preferred_element_type=jnp.float32)  7.78 us
  transfers between devices with their start and end apart: 8, of which 6 were waited for; matrix products, arithmetic and copies ran while one was open for 21% of the time, Pallas kernels for 0%

commit v1 on v0

--- a/solution.py
+++ b/solution.py
@@ -2,6 +2,22 @@
 import jax.numpy as jnp
 from jax import lax
 from jax.sharding import PartitionSpec as P
+
+
+def ring_gather(x, axis, dim):
+    ways, here, step = (lax.axis_size(axis), lax.axis_index(axis), x.shape[dim])
+    lengths = [n * ways if d == dim else n for d, n in enumerate(x.shape)]
+    full = lax.dynamic_update_slice_in_dim(jnp.zeros(lengths, x.dtype), x, here * step, axis=dim)
+    going_up = going_down = x
+    for far in range(1, ways // 2 + 1):
+        going_up = lax.ppermute(going_up, axis, [(d, (d + 1) % ways) for d in range(ways)])
+        full = lax.dynamic_update_slice_in_dim(full, going_up, (here - far) % ways * step, axis=dim)
+        if 2 * far < ways:
+            going_down = lax.ppermute(going_down, axis, [(d, (d - 1) % ways) for d in range(ways)])
+            full = lax.dynamic_update_slice_in_dim(
+                full, going_down, (here + far) % ways * step, axis=dim
+            )
+    return full
 
 
 def slot_table(route_ids, experts, capacity):
@@ -33,7 +49,7 @@
     send_grad = send_grad.reshape(experts, capacity, width)
     grouped = (
         lax.all_gather(send_in[None], "hidden", axis=0, tiled=True),
-        lax.all_gather(send_grad[None], "hidden", axis=0, tiled=True),
+        ring_gather(send_grad[None], "hidden", 0),
     )
     arrived = (
         lax.all_to_all(grouped[0], "expert", split_axis=1, concat_axis=1, tiled=True),

time: 228 us -> 217 us (0.952)
  waiting for transfers between devices: 98 us -> 75.2 us
  starting transfers between devices: 15.3 us -> 28 us
    all_gather x1, waiting for transfers between devices: 25.8 us -> 0.01 us  [on_device(): lax.all_gather(send_in[None], 'hidden', axis=0, tiled=True)]
    reduce_scatter x1, waiting for transfers between devices: 21.5 us -> 1.51 us  [on_device(): lax.psum_scatter(jnp.dot(hidden, down_w, preferred_element_type=jnp.float...]
    all_gather x1 -> x0, waiting for transfers between devices: 19.9 us -> none  [on_device(): lax.all_gather(send_grad[None], 'hidden', axis=0, tiled=True)]
    all_to_all x1, waiting for transfers between devices: 0.01 us -> 17.4 us  [on_device(): lax.all_to_all(grouped[0], 'expert', split_axis=1, concat_axis=1, tiled=T...]
    ppermute x0 -> x7, waiting for transfers between devices: none -> 16.6 us  [the longest x4 10.3 us: ring_gather(): lax.ppermute(going_up, axis, [(d, (d + 1) % ways) for d in range(ways)])]
    ppermute x0 -> x7, starting transfers between devices: none -> 11.9 us  [the longest x3 11.4 us: ring_gather(): lax.ppermute(going_down, axis, [(d, (d - 1) % ways) for d in range(ways)])]
    reduce_scatter x1, waiting for transfers between devices: 11.1 us -> 21.9 us  [on_device(): lax.psum_scatter((first + jnp.dot(grad_pre_up, up_w.T, preferred_element_...]
    dynamic_update_slice x0 -> x8, local copies, waits for them, and re-layouts: none -> 5.96 us  [the longest x4 2.98 us: ring_gather(): lax.dynamic_update_slice_in_dim(full, going_up, (here - far) % ways * ste...]
  transfers between devices with their start and end apart: 8 -> 14, of which waited for: 6 -> 10; matrix products, arithmetic and copies ran while one was open for 21% -> 27% of each run, Pallas kernels for 0% -> 0%
where the time goes in v1:
time: 217 us; the launch traced here: 216 us
  waiting for transfers between devices  75.2 us (35%)
  matrix products  73.9 us (34%)
  starting transfers between devices  28 us (13%)
  local copies, waits for them, and re-layouts  24.8 us (11%)
  between operations  13.9 us (6%)
    reduce_scatter x1, waiting for transfers between devices, on_device(): lax.psum_scatter((first + jnp.dot(grad_pre_up, up_w.T, preferred_element_...  21.9 us
    all_to_all x1, waiting for transfers between devices, on_device(): lax.all_to_all(grouped[0], 'expert', split_axis=1, concat_axis=1, tiled=T...  17.4 us
    all_to_all x1, waiting for transfers between devices, on_device(): lax.all_to_all(grouped[1], 'expert', split_axis=1, concat_axis=1, tiled=T...  13.5 us
    ppermute x3, starting transfers between devices, ring_gather(): lax.ppermute(going_down, axis, [(d, (d - 1) % ways) for d in range(ways)])  11.4 us
    ppermute x4, waiting for transfers between devices, ring_gather(): lax.ppermute(going_up, axis, [(d, (d + 1) % ways) for d in range(ways)])  10.3 us
    dot_general x1, matrix products, on_device(): first = jnp.dot(grad_pre_gate, gate_w.T, preferred_element_type=jnp.float32)  10.1 us
    dot_general x1, matrix products, on_device(): jnp.dot(grad_rows, down_w.T, preferred_element_type=jnp.float32)  9.63 us
    dot_general x1, matrix products, on_device(): jnp.dot(grad_pre_up, up_w.T, preferred_element_type=jnp.float32)  8.82 us
  transfers between devices with their start and end apart: 14, of which 10 were waited for; matrix products, arithmetic and copies ran while one was open for 27% of the time, Pallas kernels for 0%

profile of v1, /device:TPU:0, one launch (start us, length us, event | category | flops | bytes accessed | tf_op | source)
XLA Modules:
  0.0 216.1 jit_solution(9520843341958039542)
XLA Ops:
  7.2 0.8 copy.34
  8.4 0.8 copy.36
  10.3 4.1 %collective-permute-start.1 = (bf16[1,4,4,6144]{3,2,0,1:T(4,128)(2,1)S(1)}, bf16[1,4,4,6144]{3,2,0,1:T(4,128)(2,1)S(1)}, u32[]{:S(2)}, u32[]{:S(2)}) collective-permute-start(bf16[1,4,4,6144]{3,2,0,1:T(4,128)(2,1)S(1)} %bitcast.53), channel_id=1, source_target_pairs={{0,7},{1,0},{2,1},{3,2},{4,3},{5,4},{6,5},{7,6},{8,15},{9,8},{10,9... | collective-permute-start | bytes 589832 | tf_op jit(solution)/shard_map/ppermute | solution.py:16
  14.4 1.1 convolution_convert_fusion.1
  15.5 0.8 broadcast_in_dim_reshape.7
  16.3 1.9 broadcast_in_dim.16
  18.2 0.7 constant_dynamic-update-slice_fusion.7
  18.9 3.5 %collective-permute-start.3 = (bf16[1,4,4,6144]{3,2,0,1:T(4,128)(2,1)S(1)}, bf16[1,4,4,6144]{3,2,0,1:T(4,128)(2,1)S(1)}, u32[]{:S(2)}, u32[]{:S(2)}) collective-permute-start(bf16[1,4,4,6144]{3,2,0,1:T(4,128)(2,1)S(1)} %collective-permute-done.1), channel_id=1, source_target_pairs={{0,7},{1,0},{2,1},{3,2},{4,3},{5,4},{6,5},{7,6},{8,15},{9,8},{10,9... | collective-permute-start | bytes 589832 | tf_op jit(solution)/shard_map/ppermute | solution.py:16
  22.5 0.7 constant_dynamic-update-slice_fusion.6
  23.2 0.7 constant_dynamic-update-slice_fusion.5
  23.9 2.2 %collective-permute-done.2 = bf16[1,4,4,6144]{3,2,0,1:T(4,128)(2,1)S(1)} collective-permute-done((bf16[1,4,4,6144]{3,2,0,1:T(4,128)(2,1)S(1)}, bf16[1,4,4,6144]{3,2,0,1:T(4,128)(2,1)S(1)}, u32[]{:S(2)}, u32[]{:S(2)}) %collective-permute-start.2) | collective-permute-done | bytes 196640 | tf_op jit(solution)/shard_map/ppermute | solution.py:13
  26.2 3.5 %collective-permute-done.3 = bf16[1,4,4,6144]{3,2,0,1:T(4,128)(2,1)S(1)} collective-permute-done((bf16[1,4,4,6144]{3,2,0,1:T(4,128)(2,1)S(1)}, bf16[1,4,4,6144]{3,2,0,1:T(4,128)(2,1)S(1)}, u32[]{:S(2)}, u32[]{:S(2)}) %collective-permute-start.3) | collective-permute-done | bytes 196640 | tf_op jit(solution)/shard_map/ppermute | solution.py:16
  29.7 3.7 %collective-permute-start.5 = (bf16[1,4,4,6144]{3,2,0,1:T(4,128)(2,1)S(1)}, bf16[1,4,4,6144]{3,2,0,1:T(4,128)(2,1)S(1)}, u32[]{:S(2)}, u32[]{:S(2)}) collective-permute-start(bf16[1,4,4,6144]{3,2,0,1:T(4,128)(2,1)S(1)} %collective-permute-done.3), channel_id=1, source_target_pairs={{0,7},{1,0},{2,1},{3,2},{4,3},{5,4},{6,5},{7,6},{8,15},{9,8},{10,9... | collective-permute-start | bytes 589832 | tf_op jit(solution)/shard_map/ppermute | solution.py:16
  33.5 0.7 constant_dynamic-update-slice_fusion.4
  34.2 0.7 constant_dynamic-update-slice_fusion.3
  34.9 4.3 %collective-permute-done.4 = bf16[1,4,4,6144]{3,2,0,1:T(4,128)(2,1)S(1)} collective-permute-done((bf16[1,4,4,6144]{3,2,0,1:T(4,128)(2,1)S(1)}, bf16[1,4,4,6144]{3,2,0,1:T(4,128)(2,1)S(1)}, u32[]{:S(2)}, u32[]{:S(2)}) %collective-permute-start.4) | collective-permute-done | bytes 196640 | tf_op jit(solution)/shard_map/ppermute | solution.py:13
  39.3 0.7 constant_dynamic-update-slice_fusion.2
  40.0 2.8 %collective-permute-done.5 = bf16[1,4,4,6144]{3,2,0,1:T(4,128)(2,1)S(1)} collective-permute-done((bf16[1,4,4,6144]{3,2,0,1:T(4,128)(2,1)S(1)}, bf16[1,4,4,6144]{3,2,0,1:T(4,128)(2,1)S(1)}, u32[]{:S(2)}, u32[]{:S(2)}) %collective-permute-start.5) | collective-permute-done | bytes 196640 | tf_op jit(solution)/shard_map/ppermute | solution.py:16
  42.8 0.7 constant_dynamic-update-slice_fusion.1
  43.5 3.8 %collective-permute-done.6 = bf16[1,4,4,6144]{3,2,0,1:T(4,128)(2,1)S(1)} collective-permute-done((bf16[1,4,4,6144]{3,2,0,1:T(4,128)(2,1)S(1)}, bf16[1,4,4,6144]{3,2,0,1:T(4,128)(2,1)S(1)}, u32[]{:S(2)}, u32[]{:S(2)}) %collective-permute-start.6) | collective-permute-done | bytes 196640 | tf_op jit(solution)/shard_map/ppermute | solution.py:13
  47.3 0.7 constant_dynamic-update-slice_fusion
  48.0 4.2 %all-to-all-start.2 = ((bf16[8,4,4,6144]{3,2,0,1:T(4,128)(2,1)}), bf16[8,4,4,6144]{3,2,0,1:T(4,128)(2,1)S(1)}, u32[]{:S(2)}, u32[]{:S(2)}) async-start(bf16[8,4,4,6144]{3,2,0,1:T(4,128)(2,1)} %constant_dynamic-update-slice_fusion), calls=%async_computation.3 | async-start | bytes 3145728 | tf_op jit(solution)/shard_map/all_to_all | solution.py:56
  52.2 3.3 %copy.37 = bf16[8,4,4,6144]{3,2,0,1:T(4,128)(2,1)} copy(bf16[8,4,4,6144]{3,2,1,0:T(4,128)(2,1)} %all-gather.2.cloned.1.call-done) | data formatting | bytes 3145728 | tf_op jit(solution)/shard_map/all_gather | solution.py:51
  55.5 13.5 %all-to-all-done.2 = bf16[8,4,4,6144]{3,2,0,1:T(4,128)(2,1)S(1)} async-done(((bf16[8,4,4,6144]{3,2,0,1:T(4,128)(2,1)}), bf16[8,4,4,6144]{3,2,0,1:T(4,128)(2,1)S(1)}, u32[]{:S(2)}, u32[]{:S(2)}) %all-to-all-start.2) | async-done | bytes 1572896 | tf_op jit(solution)/shard_map/all_to_all | solution.py:56
  69.0 4.3 %all-to-all-start = ((bf16[8,4,4,6144]{3,2,0,1:T(4,128)(2,1)}), bf16[8,4,4,6144]{3,2,0,1:T(4,128)(2,1)}, u32[]{:S(2)}, u32[]{:S(2)}) async-start(bf16[8,4,4,6144]{3,2,0,1:T(4,128)(2,1)} %copy.37), calls=%async_computation | async-start | bytes 3145728 | tf_op jit(solution)/shard_map/all_to_all | solution.py:55
  73.5 0.7 copy.42
  74.6 17.4 %all-to-all-done = bf16[8,4,4,6144]{3,2,0,1:T(4,128)(2,1)} async-done(((bf16[8,4,4,6144]{3,2,0,1:T(4,128)(2,1)}), bf16[8,4,4,6144]{3,2,0,1:T(4,128)(2,1)}, u32[]{:S(2)}, u32[]{:S(2)}) %all-to-all-start) | async-done | bytes 1572896 | tf_op jit(solution)/shard_map/all_to_all | solution.py:55
  92.1 3.3 %copy.38 = bf16[8,4,4,6144]{3,2,1,0:T(4,128)(2,1)} copy(bf16[8,4,4,6144]{3,2,0,1:T(4,128)(2,1)} %all-to-all-done) | data formatting | bytes 3145728 | tf_op jit(solution)/shard_map/all_to_all | solution.py:55
  95.3 2.7 %reshape.48 = bf16[128,6144]{1,0:T(8,128)(2,1)S(1)} reshape(bf16[8,4,4,6144]{3,2,1,0:T(4,128)(2,1)} %copy.38) | data formatting | bytes 3145728 | tf_op jit(solution)/shard_map/reshape | solution.py:58
  98.0 6.4 %fusion.6 = f32[128,1024]{1,0:T(8,128)S(1)} fusion(bf16[128,6144]{1,0:T(8,128)(2,1)S(1)} %reshape.48, bf16[1,6144,1024]{2,1,0:T(8,128)(2,1)} %param.12), kind=kOutput, calls=%fused_computation.6 | convolution fusion | flops 1610612736 | bytes 14680064 | tf_op jit(solution)/shard_map/dot_general | solution.py:64
  104.4 6.4 %fusion.10 = f32[128,1024]{1,0:T(8,128)S(1)} fusion(bf16[128,6144]{1,0:T(8,128)(2,1)S(1)} %reshape.48, bf16[1,6144,1024]{2,1,0:T(8,128)(2,1)} %param.11), kind=kOutput, calls=%fused_computation.10 | convolution fusion | flops 1610612736 | bytes 14680064 | tf_op jit(solution)/shard_map/dot_general | solution.py:63
  110.8 9.6 %multiply_convert_fusion.1 = (bf16[128,1024]{1,0:T(8,128)(2,1)}, bf16[128,1024]{1,0:T(8,128)(2,1)S(1)}, bf16[128,1024]{1,0:T(8,128)(2,1)S(1)}) fusion(f32[128,1024]{1,0:T(8,128)S(1)} %fusion.10, f32[128,1024]{1,0:T(8,128)S(1)} %fusion.6, bf16[128,6144]{1,0:T(8,128)(2,1)S(1)} %reshape.51, bf16[1,1024,6144]{2,1,0:T(8,128)(2,1)} %param.13), kind=kOutput, calls=%fused_computation.23 | convolution fusion | flops 1612709888 | bytes 15990784 | tf_op jit(solution)/shard_map/dot_general | solution.py:78
  120.4 0.7 copy-done.3
  121.1 7.5 %fusion.18 = bf16[128,6144]{1,0:T(8,128)(2,1)} fusion(bf16[128,1024]{1,0:T(8,128)(2,1)S(1)} %get-tuple-element.8, bf16[1,1024,6144]{2,1,0:T(8,128)(2,1)} %param.13), kind=kOutput, calls=%fused_computation.17 | convolution fusion | flops 1611399168 | bytes 14417920 | tf_op jit(solution)/shard_map/dot_general | solution.py:68
  128.9 8.8 %fusion.4 = f32[128,6144]{1,0:T(8,128)S(1)} fusion(bf16[128,1024]{1,0:T(8,128)(2,1)S(1)} %get-tuple-element.9, bf16[1,6144,1024]{2,1,0:T(8,128)(2,1)} %param.12), kind=kOutput, calls=%fused_computation.4 | convolution fusion | flops 1610612736 | bytes 15990784 | tf_op jit(solution)/shard_map/dot_general | solution.py:94
  137.8 10.1 %fusion.15 = bf16[128,6144]{1,0:T(8,128)(2,1)} fusion(f32[128,6144]{1,0:T(8,128)S(1)} %fusion.4, bf16[128,1024]{1,0:T(8,128)(2,1)S(1)} %copy-done.2, bf16[1,6144,1024]{2,1,0:T(8,128)(2,1)} %param.11), kind=kOutput, calls=%fused_computation.16 | convolution fusion | flops 1612185600 | bytes 17563648 | tf_op jit(solution)/shard_map/dot_general | solution.py:92
  147.9 7.6 %convert_bitcast_fusion.2 = bf16[1,6144,1024]{2,1,0:T(8,128)(2,1)} fusion(bf16[128,6144]{1,0:T(8,128)(2,1)S(1)} %reshape.48, bf16[128,1024]{1,0:T(8,128)(2,1)} %get-tuple-element.7), kind=kOutput, calls=%fused_computation.14 | convolution fusion | flops 1616904192 | bytes 14417920 | tf_op jit(solution)/shard_map/dot_general | solution.py:86
  155.5 6.6 %convert_bitcast_fusion.1 = bf16[1,6144,1024]{2,1,0:T(8,128)(2,1)} fusion(bf16[128,6144]{1,0:T(8,128)(2,1)S(1)} %reshape.48, bf16[128,1024]{1,0:T(8,128)(2,1)S(1)} %get-tuple-element.9), kind=kOutput, calls=%fused_computation.13 | convolution fusion | flops 1616904192 | bytes 14417920 | tf_op jit(solution)/shard_map/dot_general | solution.py:89
  162.1 1.5 reduce-scatter.3.cloned.1.call-done
  163.6 1.7 reshape.49
  165.3 3.6 %all-to-all-start.1 = ((bf16[4,4,6144]{2,1,0:T(4,128)(2,1)}), bf16[4,4,6144]{2,1,0:T(4,128)(2,1)S(1)}, u32[]{:S(2)}, u32[]{:S(2)}) async-start(bf16[4,4,6144]{2,1,0:T(4,128)(2,1)} %reshape.49), calls=%async_computation.2 | async-start | bytes 393216 | tf_op jit(solution)/shard_map/all_to_all | solution.py:74
  168.8 7.6 %convert_bitcast_fusion = bf16[1,1024,6144]{2,1,0:T(8,128)(2,1)} fusion(bf16[128,1024]{1,0:T(8,128)(2,1)} %copy-done.3, bf16[128,6144]{1,0:T(8,128)(2,1)S(1)} %reshape.51), kind=kOutput, calls=%fused_computation.12 | convolution fusion | flops 1616904192 | bytes 14417920 | tf_op jit(solution)/shard_map/dot_general | solution.py:83
  176.4 21.9 %reduce-scatter.5.cloned.1.call-done = bf16[16,6144]{1,0:T(8,128)(2,1)} async-done(((bf16[128,6144]{1,0:T(8,128)(2,1)}), bf16[16,6144]{1,0:T(8,128)(2,1)}) %reduce-scatter.5.cloned.1.call-update) | async-done | bytes 196624 | tf_op jit(solution)/shard_map/reduce_scatter | solution.py:93
  198.3 1.7 reshape.52
  200.0 3.4 %all-to-all-start.3 = ((bf16[4,4,6144]{2,1,0:T(4,128)(2,1)}), bf16[4,4,6144]{2,1,0:T(4,128)(2,1)S(1)}, u32[]{:S(2)}, u32[]{:S(2)}) async-start(bf16[4,4,6144]{2,1,0:T(4,128)(2,1)} %reshape.52), calls=%async_computation.5 | async-start | bytes 393216 | tf_op jit(solution)/shard_map/all_to_all | solution.py:102
  203.5 0.9 convolution_convert_fusion.3
  204.4 4.3 %all-to-all-done.3 = bf16[4,4,6144]{2,1,0:T(4,128)(2,1)S(1)} async-done(((bf16[4,4,6144]{2,1,0:T(4,128)(2,1)}), bf16[4,4,6144]{2,1,0:T(4,128)(2,1)S(1)}, u32[]{:S(2)}, u32[]{:S(2)}) %all-to-all-start.3) | async-done | bytes 196640 | tf_op jit(solution)/shard_map/all_to_all | solution.py:102
  208.7 0.9 convolution_convert_fusion.2
  (33 shorter events, 2.6 us)
Async XLA Ops:
  7.2 2.1 copy-start
  7.2 45.1 %all-gather.2.cloned.1.call-start = ((), (), s32[]{:S(2)}) async-start(), calls=%async_computation.6 | async-start | bytes 1769472 | tf_op jit(solution)/shard_map/all_gather | solution.py:51
  9.8 9.1 %collective-permute-start = (bf16[1,4,4,6144]{3,2,0,1:T(4,128)(2,1)S(1)}, bf16[1,4,4,6144]{3,2,0,1:T(4,128)(2,1)S(1)}, u32[]{:S(2)}, u32[]{:S(2)}) collective-permute-start(bf16[1,4,4,6144]{3,2,0,1:T(4,128)(2,1)S(1)} %bitcast.52), channel_id=1, source_target_pairs={{0,1},{1,2},{2,3},{3,4},{4,5},{5,6},{6,7},{7,0},{8,9},{9,10},{10,1... | collective-permute-start | bytes 589832 | tf_op jit(solution)/shard_map/ppermute | solution.py:13
  10.3 8.6 %collective-permute-start.1 = (bf16[1,4,4,6144]{3,2,0,1:T(4,128)(2,1)S(1)}, bf16[1,4,4,6144]{3,2,0,1:T(4,128)(2,1)S(1)}, u32[]{:S(2)}, u32[]{:S(2)}) collective-permute-start(bf16[1,4,4,6144]{3,2,0,1:T(4,128)(2,1)S(1)} %bitcast.53), channel_id=1, source_target_pairs={{0,7},{1,0},{2,1},{3,2},{4,3},{5,4},{6,5},{7,6},{8,15},{9,8},{10,9... | collective-permute-start | bytes 589832 | tf_op jit(solution)/shard_map/ppermute | solution.py:16
  18.9 7.3 %collective-permute-start.2 = (bf16[1,4,4,6144]{3,2,0,1:T(4,128)(2,1)S(1)}, bf16[1,4,4,6144]{3,2,0,1:T(4,128)(2,1)S(1)}, u32[]{:S(2)}, u32[]{:S(2)}) collective-permute-start(bf16[1,4,4,6144]{3,2,0,1:T(4,128)(2,1)S(1)} %collective-permute-done), channel_id=1, source_target_pairs={{0,1},{1,2},{2,3},{3,4},{4,5},{5,6},{6,7},{7,0},{8,9},{9,10},{10,1... | collective-permute-start | bytes 589832 | tf_op jit(solution)/shard_map/ppermute | solution.py:13
  18.9 10.8 %collective-permute-start.3 = (bf16[1,4,4,6144]{3,2,0,1:T(4,128)(2,1)S(1)}, bf16[1,4,4,6144]{3,2,0,1:T(4,128)(2,1)S(1)}, u32[]{:S(2)}, u32[]{:S(2)}) collective-permute-start(bf16[1,4,4,6144]{3,2,0,1:T(4,128)(2,1)S(1)} %collective-permute-done.1), channel_id=1, source_target_pairs={{0,7},{1,0},{2,1},{3,2},{4,3},{5,4},{6,5},{7,6},{8,15},{9,8},{10,9... | collective-permute-start | bytes 589832 | tf_op jit(solution)/shard_map/ppermute | solution.py:16
  26.2 13.1 %collective-permute-start.4 = (bf16[1,4,4,6144]{3,2,0,1:T(4,128)(2,1)S(1)}, bf16[1,4,4,6144]{3,2,0,1:T(4,128)(2,1)S(1)}, u32[]{:S(2)}, u32[]{:S(2)}) collective-permute-start(bf16[1,4,4,6144]{3,2,0,1:T(4,128)(2,1)S(1)} %collective-permute-done.2), channel_id=1, source_target_pairs={{0,1},{1,2},{2,3},{3,4},{4,5},{5,6},{6,7},{7,0},{8,9},{9,10},{10,1... | collective-permute-start | bytes 589832 | tf_op jit(solution)/shard_map/ppermute | solution.py:13
  29.7 13.1 %collective-permute-start.5 = (bf16[1,4,4,6144]{3,2,0,1:T(4,128)(2,1)S(1)}, bf16[1,4,4,6144]{3,2,0,1:T(4,128)(2,1)S(1)}, u32[]{:S(2)}, u32[]{:S(2)}) collective-permute-start(bf16[1,4,4,6144]{3,2,0,1:T(4,128)(2,1)S(1)} %collective-permute-done.3), channel_id=1, source_target_pairs={{0,7},{1,0},{2,1},{3,2},{4,3},{5,4},{6,5},{7,6},{8,15},{9,8},{10,9... | collective-permute-start | bytes 589832 | tf_op jit(solution)/shard_map/ppermute | solution.py:16
  39.3 8.0 %collective-permute-start.6 = (bf16[1,4,4,6144]{3,2,0,1:T(4,128)(2,1)S(1)}, bf16[1,4,4,6144]{3,2,0,1:T(4,128)(2,1)S(1)}, u32[]{:S(2)}, u32[]{:S(2)}) collective-permute-start(bf16[1,4,4,6144]{3,2,0,1:T(4,128)(2,1)S(1)} %collective-permute-done.4), channel_id=1, source_target_pairs={{0,1},{1,2},{2,3},{3,4},{4,5},{5,6},{6,7},{7,0},{8,9},{9,10},{10,1... | collective-permute-start | bytes 589832 | tf_op jit(solution)/shard_map/ppermute | solution.py:13
  48.0 20.9 %all-to-all-start.2 = ((bf16[8,4,4,6144]{3,2,0,1:T(4,128)(2,1)}), bf16[8,4,4,6144]{3,2,0,1:T(4,128)(2,1)S(1)}, u32[]{:S(2)}, u32[]{:S(2)}) async-start(bf16[8,4,4,6144]{3,2,0,1:T(4,128)(2,1)} %constant_dynamic-update-slice_fusion), calls=%async_computation.3 | async-start | bytes 3145728 | tf_op jit(solution)/shard_map/all_to_all | solution.py:56
  69.0 23.1 %all-to-all-start = ((bf16[8,4,4,6144]{3,2,0,1:T(4,128)(2,1)}), bf16[8,4,4,6144]{3,2,0,1:T(4,128)(2,1)}, u32[]{:S(2)}, u32[]{:S(2)}) async-start(bf16[8,4,4,6144]{3,2,0,1:T(4,128)(2,1)} %copy.37), calls=%async_computation | async-start | bytes 3145728 | tf_op jit(solution)/shard_map/all_to_all | solution.py:55
  73.3 90.3 %reduce-scatter.3.cloned.1.call-start = ((), (), s32[]{:S(2)}) async-start(), calls=%async_computation.7 | async-start | bytes 1769472 | tf_op jit(solution)/shard_map/reduce_scatter | solution.py:67
  120.4 0.7 copy-start.3
  128.7 69.6 %reduce-scatter.5.cloned.1.call-start = ((), (), s32[]{:S(2)}) async-start(), calls=%async_computation.8 | async-start | bytes 1769472 | tf_op jit(solution)/shard_map/reduce_scatter | solution.py:93
  128.9 8.8 %copy-start.2 = (bf16[128,1024]{1,0:T(8,128)(2,1)S(1)}, bf16[128,1024]{1,0:T(8,128)(2,1)}, u32[]{:S(2)}) copy-start(bf16[128,1024]{1,0:T(8,128)(2,1)} %get-tuple-element.7) | copy-start | bytes 786436
  165.3 34.7 %all-to-all-start.1 = ((bf16[4,4,6144]{2,1,0:T(4,128)(2,1)}), bf16[4,4,6144]{2,1,0:T(4,128)(2,1)S(1)}, u32[]{:S(2)}, u32[]{:S(2)}) async-start(bf16[4,4,6144]{2,1,0:T(4,128)(2,1)} %reshape.49), calls=%async_computation.2 | async-start | bytes 393216 | tf_op jit(solution)/shard_map/all_to_all | solution.py:74
  168.8 40.7 %copy-start.1 = (bf16[6,6144]{1,0:T(8,128)(2,1)S(1)}, bf16[6,6144]{1,0:T(8,128)(2,1)}, u32[]{:S(2)}) copy-start(bf16[6,6144]{1,0:T(8,128)(2,1)} %param.10) | copy-start | bytes 221188
  200.0 8.6 %all-to-all-start.3 = ((bf16[4,4,6144]{2,1,0:T(4,128)(2,1)}), bf16[4,4,6144]{2,1,0:T(4,128)(2,1)S(1)}, u32[]{:S(2)}, u32[]{:S(2)}) async-start(bf16[4,4,6144]{2,1,0:T(4,128)(2,1)} %reshape.52), calls=%async_computation.5 | async-start | bytes 393216 | tf_op jit(solution)/shard_map/all_to_all | solution.py:102
Sparse Core Ops, SparseCore 0:
  16.4 29.9 all-gather.1
  128.8 34.7 reduce-scatter.2
  165.9 32.3 reduce-scatter.4
